TPU v7x, 32 devices: a whole 2x2x4 slice. The times are simulated.
32 devices in a mesh: patch: 8 (over y, x, core), mlp: 4 (over z).
Axes of the slice: x: 2, y: 2, z: 4, core: 2. Of those that a mesh axis runs over, the one named last changes fastest.
Arguments:
- latent: bfloat16 [2048, 2432], P('patch', 'mlp'), may hold values from -24 to 24
- split_list: int32 [8, 4], P('patch'), may hold values from 0 to 256, as said below
- modulation: float32 [1, 6, 2432], replicated, may hold values from -3 to 3
- w_qkv: bfloat16 [2432, 3, 1536], P(None, None, 'mlp'), may hold values from -0.125 to 0.125
- w_out: bfloat16 [1536, 2432], P('mlp'), may hold values from -0.15625 to 0.15625
- w_up: bfloat16 [2432, 5120], P(None, 'mlp'), may hold values from -0.125 to 0.125
- w_down: bfloat16 [5120, 2432], P('mlp'), may hold values from -0.078125 to 0.078125
- qk_gains: float32 [3, 64], replicated, may hold values from 1.6 to 2.4
- text_kv: bfloat16 [2, 1, 154, 1536], P(None, None, None, 'mlp'), may hold values from -6 to 6
- timestep: int32 [1], replicated, may hold values from 0 to 27
- step_sizes: float32 [28], replicated, may hold values from -0.6 to -0.1
Outputs:
- latent_next: bfloat16 [2048, 2432], P('patch', 'mlp')
Inputs may be any that keep to these rules, and one draw needn't show every extreme that they name: `split_list`: row d holds device d's tile pieces (item, count, item, count); over all devices the counts of every item add up to 1024. A device's two counts add up to at most 256, to exactly 256 on some device and to 0 on another. The devices holding an item's tokens form a run of consecutive indices of patch, taken cyclically. Both pieces may name the same item; they are then two parts of it.
All inputs are finite; a program needn't handle non-finite values.
Results may differ from a plain program's by a relative error of at most 0.0049.
Values may be sent and summed in bfloat16 or wider, within the bound.
A program may use at most 128 MiB of HBM per device.

v0:
```python
import jax
import jax.numpy as jnp
from jax import lax
from jax.sharding import PartitionSpec as P

HEAD = 64
norm_eps = 1e-06
block_rows = 512


def layer_norm(row_data):
    row_mean = jnp.mean(row_data, axis=-1, keepdims=True)
    centred = row_data - row_mean
    variance = jnp.mean(centred * centred, axis=-1, keepdims=True)
    return centred * lax.rsqrt(variance + norm_eps)


def head_norm(row_data, gain_row):
    shaped = row_data.reshape(row_data.shape[0], -1, HEAD)
    mean_square = jnp.mean(shaped * shaped, axis=-1, keepdims=True)
    return (shaped * lax.rsqrt(mean_square + norm_eps) * gain_row).reshape(row_data.shape)


def attend_dense(state_pair, queries, query_tags, key_rows, value_rows, key_tags):
    numerator, denominator = state_pair
    query_count = queries.shape[0]
    heads_here = queries.shape[1] // HEAD
    query_heads = queries.reshape(query_count, heads_here, HEAD)
    key_heads = key_rows.reshape(key_rows.shape[0], heads_here, HEAD)
    value_heads = value_rows.reshape(value_rows.shape[0], heads_here, HEAD)
    scores = jnp.einsum(
        "qhd,khd->qhk", query_heads, key_heads, preferred_element_type=jnp.float32
    ) * HEAD ** (-0.5)
    same_item = (query_tags[:, None] == key_tags[None, :])[:, None, :]
    weights = jnp.where(same_item, jnp.exp(scores), 0.0)
    denominator = denominator + jnp.sum(weights, axis=-1)
    numerator = numerator + jnp.einsum(
        "qhk,khd->qhd",
        weights.astype(jnp.bfloat16),
        value_heads,
        preferred_element_type=jnp.float32,
    )
    return (numerator, denominator)


def attend_block(state_pair, queries, query_tags, key_rows, value_rows, key_tags):
    touching = jnp.any(query_tags[:, None] == key_tags[None, :])

    def work(inner):
        return attend_dense(inner, queries, query_tags, key_rows, value_rows, key_tags)

    def skip(inner):
        return inner

    return lax.cond(touching, work, skip, state_pair)


def attend(state_pair, queries, query_tags, key_rows, value_rows, key_tags):
    key_count = key_rows.shape[0]
    if key_count > 2 * block_rows and key_count % block_rows == 0:

        def one_block(block_index, inner):
            offset = block_index * block_rows
            return attend_block(
                inner,
                queries,
                query_tags,
                lax.dynamic_slice_in_dim(key_rows, offset, block_rows, 0),
                lax.dynamic_slice_in_dim(value_rows, offset, block_rows, 0),
                lax.dynamic_slice_in_dim(key_tags, offset, block_rows, 0),
            )

        return lax.fori_loop(0, key_count // block_rows, one_block, state_pair)
    return attend_block(state_pair, queries, query_tags, key_rows, value_rows, key_tags)


def body(
    latent,
    split_list,
    modulation,
    w_qkv,
    w_out,
    w_up,
    w_down,
    qk_gains,
    text_kv,
    timestep,
    step_sizes,
):
    share_cols = latent.shape[1]
    row_data = lax.all_gather(latent, "mlp", axis=1, tiled=True)
    capacity = row_data.shape[0]
    item_total = modulation.shape[0]
    item_a = split_list[0, 0]
    count_a = split_list[0, 1]
    item_b = split_list[0, 2]
    count_b = split_list[0, 3]
    slot_ids = jnp.arange(capacity, dtype=jnp.int32)
    in_first = slot_ids < count_a
    slot_live = slot_ids < count_a + count_b
    slot_item = jnp.where(in_first, item_a, jnp.where(slot_live, item_b, -1))
    item_ids = jnp.arange(item_total, dtype=jnp.int32)
    one_hot = (slot_item[:, None] == item_ids[None, :]).astype(jnp.float32)
    slot_mods = jnp.dot(
        one_hot,
        modulation.reshape(item_total, -1),
        precision=lax.Precision.HIGHEST,
        preferred_element_type=jnp.float32,
    ).reshape(capacity, 6, -1)
    slot_step = jnp.dot(
        one_hot,
        jnp.take(step_sizes, timestep),
        precision=lax.Precision.HIGHEST,
        preferred_element_type=jnp.float32,
    )
    float_rows = row_data.astype(jnp.float32)
    normed_one = (layer_norm(float_rows) * (1.0 + slot_mods[:, 1]) + slot_mods[:, 0]).astype(
        jnp.bfloat16
    )
    projected = jnp.einsum("nd,dch->nch", normed_one, w_qkv, preferred_element_type=jnp.float32)
    queries = head_norm(projected[:, 0], qk_gains[0]).astype(jnp.bfloat16)
    key_rows = head_norm(projected[:, 1], qk_gains[1]).astype(jnp.bfloat16)
    value_rows = projected[:, 2].astype(jnp.bfloat16)
    head_cols = queries.shape[1]
    heads_here = head_cols // HEAD
    text_pair = jnp.take(text_kv, jnp.stack([item_a, item_b]), axis=1)
    text_keys = head_norm(
        text_pair[0].reshape(-1, head_cols).astype(jnp.float32), qk_gains[2]
    ).astype(jnp.bfloat16)
    text_values = text_pair[1].reshape(-1, head_cols)
    second_tag = jnp.where(item_b != item_a, item_b, -2)
    text_tags = jnp.repeat(jnp.stack([item_a, second_tag]), text_kv.shape[2]).astype(jnp.bfloat16)
    query_tags = slot_item.astype(jnp.bfloat16)
    key_tags = jnp.where(slot_live, slot_item, -3).astype(jnp.bfloat16)
    empty_state = (
        jnp.zeros((capacity, heads_here, HEAD), jnp.float32),
        jnp.zeros((capacity, heads_here), jnp.float32),
    )
    start_state = attend(empty_state, queries, query_tags, text_keys, text_values, text_tags)
    numerator, denominator = attend(
        start_state,
        queries,
        query_tags,
        lax.all_gather(key_rows, "patch", axis=0, tiled=True),
        lax.all_gather(value_rows, "patch", axis=0, tiled=True),
        lax.all_gather(key_tags, "patch", axis=0, tiled=True),
    )
    safe_denominator = denominator + (slot_item < 0).astype(jnp.float32)[:, None]
    attended = (
        (numerator / safe_denominator[:, :, None]).reshape(capacity, head_cols).astype(jnp.bfloat16)
    )
    head_part = jnp.dot(attended, w_out, preferred_element_type=jnp.float32)
    col_first = lax.axis_index("mlp") * share_cols
    attn_total = lax.psum(head_part, "mlp")
    after_attn = float_rows + slot_mods[:, 2] * attn_total
    normed_two = (layer_norm(after_attn) * (1.0 + slot_mods[:, 4]) + slot_mods[:, 3]).astype(
        jnp.bfloat16
    )
    up_total = jnp.dot(normed_two, w_up, preferred_element_type=jnp.float32)
    attn_share = lax.dynamic_slice_in_dim(after_attn, col_first, share_cols, 1)
    hidden_units = jax.nn.gelu(up_total, approximate=True).astype(jnp.bfloat16)
    unit_part = jnp.dot(hidden_units, w_down, preferred_element_type=jnp.float32)
    unit_total = lax.psum_scatter(unit_part, "mlp", scatter_dimension=1, tiled=True)
    gate_share = lax.dynamic_slice_in_dim(slot_mods[:, 5], col_first, share_cols, 1)
    after_mlp = attn_share + gate_share * unit_total
    next_rows = latent.astype(jnp.float32) + slot_step[:, None] * after_mlp
    return jnp.where(slot_live[:, None], next_rows, 0.0).astype(jnp.bfloat16)


def solution(mesh):
    return jax.shard_map(
        body,
        mesh=mesh,
        in_specs=(
            P("patch", "mlp"),
            P("patch", None),
            P(),
            P(None, None, "mlp"),
            P("mlp", None),
            P(None, "mlp"),
            P("mlp", None),
            P(),
            P(None, None, None, "mlp"),
            P(),
            P(),
        ),
        out_specs=P("patch", "mlp"),
        check_vma=False,
    )
```

profile of v0, /device:TPU:0, one launch (start us, length us, event | category | flops | bytes accessed | tf_op | source)
XLA Modules:
  0.0 319.1 jit_solution(8434744912893777445)
XLA Ops:
  15.4 6.1 %broadcast_multiply_fusion = f32[256,6,2432]{0,2,1:T(8,128)} fusion(f32[6,2432]{1,0:T(8,128)S(1)} %bitcast.153, f32[256]{0:T(256)S(1)} %get-tuple-element.424), kind=kLoop, calls=%fused_computation.23 | loop fusion | flops 3735552 | bytes 15001600 | tf_op jit(solution)/shard_map/dot_general | solution.py:104
  21.6 21.7 %all-gather.6.cloned.1.call-done = bf16[256,2432]{0,1:T(8,128)(2,1)} async-done(((bf16[256,608]{0,1:T(8,128)(2,1)}), bf16[256,2432]{0,1:T(8,128)(2,1)}) %all-gather.6.cloned.1.call-update) | async-done | bytes 1245200 | tf_op jit(solution)/shard_map/all_gather | solution.py:91
  46.7 6.0 %fusion.44 = f32[256,3,384]{2,0,1:T(8,128)S(1)} fusion(bf16[2432,3,384]{2,0,1:T(8,128)(2,1)} %param.20, f32[256,6,2432]{0,2,1:T(8,128)} %broadcast_multiply_fusion, bf16[256,2432]{0,1:T(8,128)(2,1)S(1)} %copy-done.2, f32[256]{0:T(256)S(1)} %add_rsqrt_fusion.4, f32[256]{0:T(256)S(1)} %broadcast_multiply_fusion.2), kind=kOutput, calls=%fused_computation.58 | convolution fusion | flops 1438810112 | bytes 13010944 | tf_op jit(solution)/shard_map/nd,dch->nch/dot_general | solution.py:120
  61.2 2.1 fusion.60
  75.1 2.6 reshape.303
  79.7 2.2 fusion.63
  81.9 2.6 mul.193
  86.5 2.1 copy.95
  88.7 9.0 %all-gather.1 = bf16[8,1,256]{2,1,0:T(2,128)(2,1)S(1)} all-gather(bf16[1,1,256]{2,1,0:T(2,128)(2,1)S(1)} %reshape.300), channel_id=1, replica_groups=mesh['patch'=8,'mlp'=4] {'patch'}, dimensions={0}, use_global_device_ids=true | all-gather | bytes 4608 | tf_op jit(solution)/shard_map/all_gather | solution.py:146
  100.5 8.4 %conditional.2 = (f32[256,6,64]{0,2,1:T(8,128)S(1)}, f32[256,6]{0,1:T(8,128)S(1)}) conditional(s32[]{:T(128)} %convert_element_type.111, () %tuple.38, (bf16[256]{0:T(256)(128)(2,1)S(1)}, s32[2]{0:T(128)S(1)}, bf16[308,384]{1,0:T(8,128)(2,1)}, bf16[256,384]{1,0:T(8,128)(2,1)S(1)}, bf16[2,2,154,384]{2,1,3,0:T(2,128)(2,1)}) %tuple.110), branch_computations={%region_5.6_spmd, %region_6.8_spmd} | conditional | flops 123080192 | bytes 5880796 | solution.py:55
  108.9 2.6 copy.105
  111.5 2.6 copy.103
  114.1 29.6 %while.17 = (s32[]{:T(128)}, f32[256,6,64]{0,2,1:T(8,128)S(1)}, f32[256,6]{0,1:T(8,128)S(1)}, bf16[2048]{0:T(1024)(128)(2,1)S(1)}, bf16[2048,384]{0,1:T(8,128)(2...) while((s32[]{:T(128)}, f32[256,6,64]{0,2,1:T(8,128)S(1)}, ...), condition=%wide.region_14.15_spmd.clone, body=%wide.region_9.14_spmd.clone.sunk | while | flops 206537984 | bytes 10057545 | solution.py:73
  117.6 3.9 %conditional.5 = ((f32[256,6,64]{0,2,1:T(8,128)S(1)}, f32[256,6]{0,1:T(8,128)S(1)})) conditional(s32[]{:T(128)} %convert_element_type.190, (f32[256,6,64]{0,2,1:T(8,128)S(1)}, f32[256,6]{0,1:T(8,128)S(1)}) %tuple.89, (bf16[256]{0:T(256)(128)(2,1)S(1)}, bf16[512]{0:T(512)(128)(2,1)S(1)}, bf16[2048,384]{0,1:T(8,128)(2,1)}, s32[]{:T(128)}, ...), branch_computations={%region_11.11_spmd, %region_12.13_spmd} | conditional | flops 206274560 | bytes 10053148 | solution.py:55
  125.0 3.9 %conditional.5 = ((f32[256,6,64]{0,2,1:T(8,128)S(1)}, f32[256,6]{0,1:T(8,128)S(1)})) conditional(s32[]{:T(128)} %convert_element_type.190, (f32[256,6,64]{0,2,1:T(8,128)S(1)}, f32[256,6]{0,1:T(8,128)S(1)}) %tuple.89, (bf16[256]{0:T(256)(128)(2,1)S(1)}, bf16[512]{0:T(512)(128)(2,1)S(1)}, bf16[2048,384]{0,1:T(8,128)(2,1)}, s32[]{:T(128)}, ...), branch_computations={%region_11.11_spmd, %region_12.13_spmd} | conditional | flops 206274560 | bytes 10053148 | solution.py:55
  132.4 3.9 %conditional.5 = ((f32[256,6,64]{0,2,1:T(8,128)S(1)}, f32[256,6]{0,1:T(8,128)S(1)})) conditional(s32[]{:T(128)} %convert_element_type.190, (f32[256,6,64]{0,2,1:T(8,128)S(1)}, f32[256,6]{0,1:T(8,128)S(1)}) %tuple.89, (bf16[256]{0:T(256)(128)(2,1)S(1)}, bf16[512]{0:T(512)(128)(2,1)S(1)}, bf16[2048,384]{0,1:T(8,128)(2,1)}, s32[]{:T(128)}, ...), branch_computations={%region_11.11_spmd, %region_12.13_spmd} | conditional | flops 206274560 | bytes 10053148 | solution.py:55
  139.8 3.9 %conditional.5 = ((f32[256,6,64]{0,2,1:T(8,128)S(1)}, f32[256,6]{0,1:T(8,128)S(1)})) conditional(s32[]{:T(128)} %convert_element_type.190, (f32[256,6,64]{0,2,1:T(8,128)S(1)}, f32[256,6]{0,1:T(8,128)S(1)}) %tuple.89, (bf16[256]{0:T(256)(128)(2,1)S(1)}, bf16[512]{0:T(512)(128)(2,1)S(1)}, bf16[2048,384]{0,1:T(8,128)(2,1)}, s32[]{:T(128)}, ...), branch_computations={%region_11.11_spmd, %region_12.13_spmd} | conditional | flops 206274560 | bytes 10053148 | solution.py:55
  143.8 2.4 fusion.75
  146.3 98.0 %all-reduce.2.cloned.1.call-done = f32[256,2432]{0,1:T(8,128)} async-done(((f32[256,2432]{0,1:T(8,128)}), f32[256,2432]{0,1:T(8,128)}) %all-reduce.2.cloned.1.call-update) | async-done | bytes 2490384 | tf_op jit(solution)/shard_map/psum | solution.py:154
  244.3 2.9 fusion.71
  249.0 12.0 %convolution_bitcast_fusion.1 = f32[2432,256]{1,0:T(8,128)} fusion(bf16[1280,2432]{1,0:T(8,128)(2,1)} %param.23, bf16[2432,1280]{1,0:T(8,128)(2,1)} %param.22, f32[256,6,2432]{0,2,1:T(8,128)} %broadcast_multiply_fusion, f32[256,2432]{0,1:T(8,128)} %copy-done.1, f32[256]{0:T(256)S(1)} %add_rsqrt_fusion.3, f32[256]{0:T(256)S(1)} %broadcast_multiply_fusion.1), kind=kOutput, calls=%fused_computation.24 | convolution fusion | flops 3194355712 | bytes 22415360
  261.0 3.4 %slice.85 = f32[256,1,2432]{0,2,1:T(8,128)} slice(f32[256,6,2432]{0,2,1:T(8,128)} %broadcast_multiply_fusion), slice={[0:256], [5:6], [0:2432]} | slice | bytes 4980736 | tf_op jit(solution)/shard_map/slice | solution.py:164
  264.4 45.9 %reduce-scatter.4.cloned.1.call-done = f32[608,256]{1,0:T(8,128)} async-done(((f32[2432,256]{1,0:T(8,128)}), f32[608,256]{1,0:T(8,128)}) %reduce-scatter.4.cloned.1.call-update) | async-done | bytes 622608
  310.3 2.3 fusion.58
  (122 shorter events, 70.9 us)
Async XLA Ops:
  6.5 137.3 %copy-start = (bf16[384,2432]{1,0:T(8,128)(2,1)S(1)}, bf16[384,2432]{1,0:T(8,128)(2,1)}, u32[]{:S(2)}) copy-start(bf16[384,2432]{1,0:T(8,128)(2,1)} %param.21) | copy-start | bytes 5603332
  6.5 36.7 %all-gather.6.cloned.1.call-start = ((), (), s32[]{:S(2)}) async-start(), calls=%async_computation.1 | async-start | bytes 1556480 | tf_op jit(solution)/shard_map/all_gather | solution.py:91
  7.3 101.7 %all-gather.10.cloned.1.call-start = ((), (), s32[]{:S(2)}) async-start(), calls=%async_computation.4 | async-start | bytes 1769472 | tf_op jit(solution)/shard_map/all_gather | solution.py:145
  43.2 3.4 %copy-start.2 = (bf16[256,2432]{0,1:T(8,128)(2,1)S(1)}, bf16[256,2432]{0,1:T(8,128)(2,1)}, u32[]{:S(2)}) copy-start(bf16[256,2432]{0,1:T(8,128)(2,1)} %all-gather.6.cloned.1.call-done) | copy-start | bytes 3735556
  46.7 7.9 %copy-start.7 = (f32[3,64]{1,0:T(4,128)S(1)}, f32[3,64]{1,0:T(4,128)}, u32[]{:S(2)}) copy-start(f32[3,64]{1,0:T(4,128)} %param.24) | copy-start | bytes 2308
  52.7 1.0 copy-start.4
  54.5 57.1 %all-gather.8.cloned.1.call-start = ((), (), s32[]{:S(2)}) async-start(), calls=%async_computation.2 | async-start | bytes 1769472 | tf_op jit(solution)/shard_map/all_gather | solution.py:144
  63.3 181.0 %all-reduce.2.cloned.1.call-start = ((), (), s32[]{:S(2)}) async-start(), calls=%async_computation.3 | async-start | bytes 4980736 | tf_op jit(solution)/shard_map/psum | solution.py:154
  72.9 0.9 copy-start.3
  106.6 1.7 copy-start.6
  146.3 164.0 %reduce-scatter.4.cloned.1.call-start = ((), (), s32[]{:S(2)}) async-start(), calls=%async_computation.5 | async-start | bytes 3112960
  247.2 1.4 copy-start.1
  261.0 49.3 %copy-start.5 = (bf16[256,608]{0,1:T(8,128)(2,1)S(1)}, bf16[256,608]{0,1:T(8,128)(2,1)}, u32[]{:S(2)}) copy-start(bf16[256,608]{0,1:T(8,128)(2,1)} %param.17) | copy-start | bytes 933892
Sparse Core Ops, SparseCore 0:
  8.9 34.2 all-gather.5
  54.6 24.7 all-gather.9
  81.3 25.7 all-gather.7
  146.4 97.8 all-reduce.1
  261.1 49.0 reduce-scatter.3
where the time goes:
time: 321 us; the launch traced here: 319 us
  waiting for transfers between devices  166 us (52%)
  local copies, waits for them, and re-layouts  45.1 us (14%)
  other arithmetic  44.3 us (14%)
  matrix products  32.5 us (10%)
  between operations  18.6 us (6%)
  blocking collectives  9.01 us (3%)
    psum x1, waiting for transfers between devices, body(): attn_total = lax.psum(head_part, 'mlp')  98 us
    unnamed x6, waiting for transfers between devices  46.6 us
    all_gather x1, waiting for transfers between devices, body(): row_data = lax.all_gather(latent, 'mlp', axis=1, tiled=True)  21.7 us
    unnamed x1, matrix products  12 us
    unnamed x20, local copies, waits for them, and re-layouts  10.3 us
    all_gather x1, blocking collectives, body(): lax.all_gather(key_tags, 'patch', axis=0, tiled=True)  9.01 us
    dot_general x5, matrix products, attend_dense(): jnp.einsum('qhd,khd->qhk', query_heads, key_heads, preferred_element_type...  8.96 us
    convert_element_type x4, other arithmetic, body(): query_tags = slot_item.astype(jnp.bfloat16)  7.74 us
  transfers between devices with their start and end apart: 5, of which 3 were waited for; matrix products, arithmetic and copies ran while one was open for 18% of the time, Pallas kernels for 0%

commit v1 on v0

--- a/solution.py
+++ b/solution.py
@@ -151,7 +151,7 @@
     )
     head_part = jnp.dot(attended, w_out, preferred_element_type=jnp.float32)
     col_first = lax.axis_index("mlp") * share_cols
-    attn_total = lax.psum(head_part, "mlp")
+    attn_total = jnp.sum(lax.all_gather(head_part, "mlp"), axis=0)
     after_attn = float_rows + slot_mods[:, 2] * attn_total
     normed_two = (layer_norm(after_attn) * (1.0 + slot_mods[:, 4]) + slot_mods[:, 3]).astype(
         jnp.bfloat16

time: 321 us -> 403 us (1.26)
  waiting for transfers between devices: 166 us -> 241 us
  other arithmetic: 44.3 us -> 49.9 us
    all_gather x0 -> x1, waiting for transfers between devices: none -> 174 us  [body(): attn_total = jnp.sum(lax.all_gather(head_part, 'mlp'), axis=0)]
    psum x1 -> x0, waiting for transfers between devices: 98 us -> none  [body(): attn_total = lax.psum(head_part, 'mlp')]
    unnamed x6 -> x5, waiting for transfers between devices: 46.6 us -> 0.78 us
    reduce_scatter x0 -> x1, waiting for transfers between devices: none -> 45 us  [body(): lax.psum_scatter(unit_part, 'mlp', scatter_dimension=1, tiled=True)]
    unnamed x1 -> x0, matrix products: 12 us -> none
    dot_general x0 -> x1, matrix products: none -> 12 us  [body(): jnp.dot(hidden_units, w_down, preferred_element_type=jnp.float32)]
    reduce_sum x0 -> x1, other arithmetic: none -> 6.14 us  [body(): attn_total = jnp.sum(lax.all_gather(head_part, 'mlp'), axis=0)]
  transfers between devices with their start and end apart: 5 -> 5, of which waited for: 3 -> 3; matrix products, arithmetic and copies ran while one was open for 18% -> 15% of each run, Pallas kernels for 0% -> 0%
where the time goes in v1:
time: 403 us; the launch traced here: 402 us
  waiting for transfers between devices  241 us (60%)
  other arithmetic  49.9 us (12%)
  local copies, waits for them, and re-layouts  45.4 us (11%)
  matrix products  34.7 us (9%)
  between operations  18.5 us (5%)
  blocking collectives  8.89 us (2%)
    all_gather x1, waiting for transfers between devices, body(): attn_total = jnp.sum(lax.all_gather(head_part, 'mlp'), axis=0)  174 us
    reduce_scatter x1, waiting for transfers between devices, body(): lax.psum_scatter(unit_part, 'mlp', scatter_dimension=1, tiled=True)  45 us
    all_gather x1, waiting for transfers between devices, body(): row_data = lax.all_gather(latent, 'mlp', axis=1, tiled=True)  21.9 us
    dot_general x1, matrix products, body(): jnp.dot(hidden_units, w_down, preferred_element_type=jnp.float32)  12 us
    unnamed x20, local copies, waits for them, and re-layouts  10.2 us
    dot_general x5, matrix products, attend_dense(): jnp.einsum('qhd,khd->qhk', query_heads, key_heads, preferred_element_type...  9.97 us
    all_gather x1, blocking collectives, body(): lax.all_gather(key_tags, 'patch', axis=0, tiled=True)  8.89 us
  transfers between devices with their start and end apart: 5, of which 3 were waited for; matrix products, arithmetic and copies ran while one was open for 15% of the time, Pallas kernels for 0%

profile of v1, /device:TPU:0, one launch (start us, length us, event | category | flops | bytes accessed | tf_op | source)
XLA Modules:
  0.0 401.8 jit_solution(10094006613317877785)
XLA Ops:
  15.2 6.1 %broadcast_multiply_fusion = f32[256,6,2432]{0,2,1:T(8,128)} fusion(f32[6,2432]{1,0:T(8,128)S(1)} %bitcast.151, f32[256]{0:T(256)S(1)} %get-tuple-element.408), kind=kLoop, calls=%fused_computation.23 | loop fusion | flops 3735552 | bytes 15001600 | tf_op jit(solution)/shard_map/dot_general | solution.py:104
  21.4 21.9 %all-gather.8.cloned.1.call-done = bf16[256,2432]{0,1:T(8,128)(2,1)} async-done(((bf16[256,608]{0,1:T(8,128)(2,1)}), bf16[256,2432]{0,1:T(8,128)(2,1)}) %all-gather.8.cloned.1.call-update) | async-done | bytes 1245200 | tf_op jit(solution)/shard_map/all_gather | solution.py:91
  46.7 6.0 %fusion.44 = f32[256,3,384]{2,0,1:T(8,128)S(1)} fusion(bf16[2432,3,384]{2,0,1:T(8,128)(2,1)} %param.20, f32[256,6,2432]{0,2,1:T(8,128)} %broadcast_multiply_fusion, bf16[256,2432]{0,1:T(8,128)(2,1)S(1)} %copy-done.2, f32[256]{0:T(256)S(1)} %add_rsqrt_fusion.4, f32[256]{0:T(256)S(1)} %broadcast_multiply_fusion.2), kind=kOutput, calls=%fused_computation.57 | convolution fusion | flops 1438810112 | bytes 13010944 | tf_op jit(solution)/shard_map/nd,dch->nch/dot_general | solution.py:120
  71.9 2.6 mul.193
  80.8 2.6 reshape.304
  88.6 8.9 %all-gather.2 = bf16[8,1,256]{2,1,0:T(2,128)(2,1)S(1)} all-gather(bf16[1,1,256]{2,1,0:T(2,128)(2,1)S(1)} %reshape.301), channel_id=1, replica_groups=mesh['patch'=8,'mlp'=4] {'patch'}, dimensions={0}, use_global_device_ids=true | all-gather | bytes 4608 | tf_op jit(solution)/shard_map/all_gather | solution.py:146
  100.2 7.9 %conditional.2 = (f32[256,6,64]{0,2,1:T(8,128)S(1)}, f32[256,6]{0,1:T(8,128)S(1)}) conditional(s32[]{:T(128)} %convert_element_type.111, () %tuple.38, (bf16[256]{0:T(256)(128)(2,1)S(1)}, s32[2]{0:T(128)S(1)}, bf16[308,384]{1,0:T(8,128)(2,1)}, bf16[256,384]{1,0:T(8,128)(2,1)S(1)}, bf16[2,2,154,384]{2,1,3,0:T(2,128)(2,1)}) %tuple.108), branch_computations={%region_5.6_spmd, %region_6.8_spmd} | conditional | flops 123080192 | bytes 6826972 | solution.py:55
  102.5 2.7 fusion.74
  108.2 2.6 copy.77
  110.8 2.6 copy.75
  113.4 28.8 %while.17 = (s32[]{:T(128)}, f32[256,6,64]{0,2,1:T(8,128)S(1)}, f32[256,6]{0,1:T(8,128)S(1)}, bf16[2048]{0:T(1024)(128)(2,1)S(1)}, bf16[2048,384]{0,1:T(8,128)(2...) while((s32[]{:T(128)}, f32[256,6,64]{0,2,1:T(8,128)S(1)}, ...), condition=%wide.region_14.15_spmd.clone, body=%wide.region_9.14_spmd.clone.sunk | while | flops 206537984 | bytes 10057537 | solution.py:73
  116.7 3.9 conditional.5
  123.9 3.9 conditional.5
  131.1 3.9 conditional.5
  138.3 3.9 conditional.5
  142.3 2.4 fusion.76
  144.7 173.8 %all-gather.14.cloned.1.call-done = f32[1024,2432]{1,0:T(8,128)} async-done(((f32[256,2432]{1,0:T(8,128)}), f32[1024,2432]{1,0:T(8,128)}) %all-gather.14.cloned.1.call-update) | async-done | bytes 9961488 | tf_op jit(solution)/shard_map/all_gather | solution.py:154
  318.5 6.1 %reduce_sum.97 = f32[256,2432]{1,0:T(8,128)} reduce(f32[4,256,2432]{2,1,0:T(8,128)} %bitcast.142, f32[]{:T(128)} %constant.118.clone.1), dimensions={0}, to_apply=%region_15.16 | reduce | flops 1867776 | bytes 12451844 | tf_op jit(solution)/shard_map/reduce_sum | solution.py:154
  324.7 3.2 copy.78
  327.9 2.9 fusion.72
  332.5 12.0 %fusion.53 = f32[256,2432]{0,1:T(8,128)} fusion(bf16[1280,2432]{1,0:T(8,128)(2,1)} %param.23, bf16[2432,1280]{1,0:T(8,128)(2,1)} %param.22, f32[256,6,2432]{0,2,1:T(8,128)} %broadcast_multiply_fusion, f32[256,2432]{0,1:T(8,128)} %copy-done.1, f32[256]{0:T(256)S(1)} %add_rsqrt_fusion.3, f32[256]{0:T(256)S(1)} %broadcast_multiply_fusion.1), kind=kOutput, calls=%fused_computation.64 | convolution fusion | flops 3194355712 | bytes 22415360 | tf_op jit(solution)/shard_map/dot_general | solution.py:162
  344.6 3.4 slice.85
  348.0 45.0 %reduce-scatter.2.cloned.1.call-done = f32[256,608]{0,1:T(8,128)} async-done(((f32[256,2432]{0,1:T(8,128)}), f32[256,608]{0,1:T(8,128)}) %reduce-scatter.2.cloned.1.call-update) | async-done | bytes 622608 | tf_op jit(solution)/shard_map/reduce_scatter | solution.py:163
  393.0 2.3 fusion.59
  (124 shorter events, 73.5 us)
Async XLA Ops:
  6.5 135.8 %copy-start = (bf16[384,2432]{1,0:T(8,128)(2,1)S(1)}, bf16[384,2432]{1,0:T(8,128)(2,1)}, u32[]{:S(2)}) copy-start(bf16[384,2432]{1,0:T(8,128)(2,1)} %param.21) | copy-start | bytes 5603332
  6.5 36.7 %all-gather.8.cloned.1.call-start = ((), (), s32[]{:S(2)}) async-start(), calls=%async_computation.1 | async-start | bytes 1556480 | tf_op jit(solution)/shard_map/all_gather | solution.py:91
  7.3 100.9 %all-gather.12.cloned.1.call-start = ((), (), s32[]{:S(2)}) async-start(), calls=%async_computation.4 | async-start | bytes 1769472 | tf_op jit(solution)/shard_map/all_gather | solution.py:145
  43.2 3.4 copy-start.2
  46.7 7.9 %copy-start.7 = (f32[3,64]{1,0:T(4,128)S(1)}, f32[3,64]{1,0:T(4,128)}, u32[]{:S(2)}) copy-start(f32[3,64]{1,0:T(4,128)} %param.24) | copy-start | bytes 2308
  52.7 1.0 copy-start.5
  54.5 56.3 %all-gather.10.cloned.1.call-start = ((), (), s32[]{:S(2)}) async-start(), calls=%async_computation.2 | async-start | bytes 1769472 | tf_op jit(solution)/shard_map/all_gather | solution.py:144
  63.3 255.2 %all-gather.14.cloned.1.call-start = ((), (), s32[]{:S(2)}) async-start(), calls=%async_computation.5 | async-start | bytes 12451840 | tf_op jit(solution)/shard_map/all_gather | solution.py:154
  69.8 0.9 copy-start.3
  102.4 2.8 copy-start.4
  144.7 248.3 %reduce-scatter.2.cloned.1.call-start = ((), (), s32[]{:S(2)}) async-start(), calls=%async_computation.3 | async-start | bytes 3112960 | tf_op jit(solution)/shard_map/reduce_scatter | solution.py:163
  330.7 1.4 copy-start.1
  344.6 48.4 %copy-start.6 = (bf16[256,608]{0,1:T(8,128)(2,1)S(1)}, bf16[256,608]{0,1:T(8,128)(2,1)}, u32[]{:S(2)}) copy-start(bf16[256,608]{0,1:T(8,128)(2,1)} %param.17) | copy-start | bytes 933892
Sparse Core Ops, SparseCore 0:
  8.9 34.2 all-gather.7
  54.6 24.7 all-gather.11
  81.3 25.7 all-gather.9
  144.8 173.6 all-gather.13
  344.7 48.2 reduce-scatter.1
